TPU v7x, 32 devices: a whole 2x2x4 slice. The times are simulated.
32 devices in a mesh: row: 8 (over z, core), col: 4 (over y, x).
Axes of the slice: x: 2, y: 2, z: 4, core: 2. Of those that a mesh axis runs over, the one named last changes fastest.
Arguments:
- token_ids: int32 [16, 256], P('row'), may hold values from 0 to 16383
- passage_lengths: int32 [16], P('row'), may hold values from 64 to 256, as said below
- embedding: bfloat16 [16384, 4096], P(None, 'col'), may hold values from -8 to 8
- attn_gain: bfloat16 [4096], P('col'), may hold values from 0.25 to 1.75
- final_gain: bfloat16 [4096], P('col'), may hold values from 0.25 to 1.75
- query_weight: bfloat16 [4096, 4096], P('row', 'col'), may hold values from -0.5 to 0.5
- key_weight: bfloat16 [4096, 4096], P('row', 'col'), may hold values from -0.5 to 0.5
- value_weight: bfloat16 [4096, 4096], P('row', 'col'), may hold values from -0.09375 to 0.09375
- out_weight: bfloat16 [4096, 4096], P('row', 'col'), may hold values from -0.09375 to 0.09375
- crosskey_weight: bfloat16 [4096, 4096], P('row', 'col'), may hold values from -0.09375 to 0.09375
- crossvalue_weight: bfloat16 [4096, 4096], P('row', 'col'), may hold values from -0.09375 to 0.09375
Outputs:
- hidden_out: bfloat16 [4096, 4096], P('row', 'col')
- cross_keys: bfloat16 [4096, 16, 256], P('row', 'col')
- cross_values: bfloat16 [4096, 16, 256], P('row', 'col')
Inputs may be any that keep to these rules, and one draw needn't show every extreme that they name: `passage_lengths`: some passage of every draw has all 256 slots valid.
All inputs are finite; a program needn't handle non-finite values.
Results may differ from a plain program's by a relative error of at most 0.0082.
Values may be sent and summed in bfloat16 or wider, within the bound.
A program may use at most 128 MiB of HBM per device.

v0:
```python
import jax
import jax.numpy as jnp
from jax import lax
from jax.sharding import PartitionSpec as P

D = 4096
HD = 256
PLEN = 256


epsilon = 1e-06
masked_score = -1000000000.0


def scaled_rows(widened, summed, gain_row):
    inverse = lax.rsqrt(summed / D + epsilon)
    return (widened * inverse * gain_row.astype(jnp.float32)).astype(jnp.bfloat16)


def spread_norm(row_block, gain_row, which):
    if which == 0:
        gathered, gains = (
            lax.all_gather(row_block, "col", axis=1, tiled=True),
            lax.all_gather(gain_row.reshape(1, -1), "col", axis=1, tiled=True),
        )
    else:
        gathered, gains = (
            lax.all_gather(row_block, "col", axis=1, tiled=True),
            lax.all_gather(gain_row.reshape(1, -1), "col", axis=1, tiled=True),
        )
    widened = gathered.astype(jnp.float32)
    summed = jnp.sum(widened * widened, axis=1, keepdims=True)
    return scaled_rows(widened, summed, gains)


def add_terms(source, pieces):
    return tuple(
        (
            jnp.dot(source, weight_piece, preferred_element_type=jnp.float32)
            for weight_piece in pieces
        )
    )


def attend(query_rows, key_rows, value_rows, passage_lengths):
    tok_rows, local_width = query_rows.shape
    passages_here = tok_rows // PLEN
    heads_here = local_width // HD
    query_four = query_rows.reshape(passages_here, PLEN, heads_here, HD)
    key_four = key_rows.reshape(passages_here, PLEN, heads_here, HD)
    value_four = value_rows.reshape(passages_here, PLEN, heads_here, HD)
    scores = jnp.einsum(
        "pihd,pjhd->phij", query_four, key_four, preferred_element_type=jnp.float32
    ) * HD ** (-0.5)
    valid = jnp.arange(PLEN, dtype=jnp.int32)[None, :] < passage_lengths[:, None]
    scores = jnp.where(valid[:, None, None, :], scores, masked_score)
    highest = jnp.max(scores, axis=-1, keepdims=True)
    expon = jnp.exp(scores - highest)
    probs = (expon / jnp.sum(expon, axis=-1, keepdims=True)).astype(jnp.bfloat16)
    mixed = jnp.einsum("phij,pjhd->pihd", probs, value_four, preferred_element_type=jnp.float32)
    return mixed.astype(jnp.bfloat16).reshape(tok_rows, local_width)


def shards(
    token_ids,
    passage_lengths,
    embedding,
    attn_gain,
    final_gain,
    query_weight,
    key_weight,
    value_weight,
    out_weight,
    crosskey_weight,
    crossvalue_weight,
):
    embedded = jnp.take(embedding, token_ids.reshape(-1), axis=0)
    normed = spread_norm(embedded, attn_gain, 0)
    tok_rows = normed.shape[0]
    local_width = query_weight.shape[1]
    query_sum, key_sum, value_sum = add_terms(
        normed,
        (
            lax.all_gather(query_weight, "row", axis=0, tiled=True),
            lax.all_gather(key_weight, "row", axis=0, tiled=True),
            lax.all_gather(value_weight, "row", axis=0, tiled=True),
        ),
    )
    attended = attend(
        query_sum.astype(jnp.bfloat16),
        key_sum.astype(jnp.bfloat16),
        value_sum.astype(jnp.bfloat16),
        passage_lengths,
    )
    heads_full = lax.all_gather(attended, "col", axis=1, tiled=True)
    (projected,) = add_terms(heads_full, (lax.all_gather(out_weight, "row", axis=0, tiled=True),))
    hidden_out = (embedded.astype(jnp.float32) + projected).astype(jnp.bfloat16)
    final_normed = spread_norm(hidden_out, final_gain, 1)
    crosskey_sum, crossvalue_sum = add_terms(
        final_normed,
        (
            lax.all_gather(crosskey_weight, "row", axis=0, tiled=True),
            lax.all_gather(crossvalue_weight, "row", axis=0, tiled=True),
        ),
    )
    heads_here = local_width // HD
    cross_keys = crosskey_sum.astype(jnp.bfloat16).reshape(tok_rows, heads_here, HD)
    cross_values = crossvalue_sum.astype(jnp.bfloat16).reshape(tok_rows, heads_here, HD)
    return (hidden_out, cross_keys, cross_values)


def solution(mesh):
    return jax.shard_map(
        shards,
        mesh=mesh,
        in_specs=(
            P("row", None),
            P("row"),
            P(None, "col"),
            P("col"),
            P("col"),
            P("row", "col"),
            P("row", "col"),
            P("row", "col"),
            P("row", "col"),
            P("row", "col"),
            P("row", "col"),
        ),
        out_specs=(P("row", "col"), P("row", "col", None), P("row", "col", None)),
        check_vma=False,
    )
```

profile of v0, /device:TPU:24, one launch (start us, length us, event | category | flops | bytes accessed | tf_op | source)
XLA Modules:
  0.0 695.9 jit_solution(5520122461572180474)
XLA Ops:
  7.2 0.0 all-gather.12.cloned.1.call-start
  7.2 0.7 copy.30
  7.9 0.7 copy.29
  8.6 5.1 gather_fusion
  13.7 1.1 broadcast_select_fusion
  14.9 0.0 all-gather.14.cloned.1.call-start
  15.0 0.7 all-gather.14.cloned.1.call-update
  15.7 0.0 all-gather.18.cloned.1.call-start
  15.7 0.7 all-gather.18.cloned.1.call-update
  16.4 0.0 all-gather.16.cloned.1.call-start
  16.4 0.5 all-gather.16.cloned.1.call-update
  17.0 0.5 all-gather.22.cloned.1.call-update
  17.6 0.0 all-gather.20.cloned.1.call-start
  17.6 8.1 %all-gather = bf16[4096]{0:T(1024)(128)(2,1)S(1)} all-gather(bf16[1024]{0:T(1024)(128)(2,1)S(1)} %copy-done.1), channel_id=2, replica_groups=mesh['row'=8,'col'=4] {'col'}, dimensions={0}, use_global_device_ids=true | all-gather | bytes 10240 | tf_op jit(solution)/shard_map/all_gather | solution.py:24
  25.7 0.1 iota_compare_fusion
  25.8 43.0 %all-gather.12.cloned.1.call-done = bf16[512,4096]{1,0:T(8,128)(2,1)} async-done(((bf16[512,1024]{1,0:T(8,128)(2,1)}), bf16[512,4096]{1,0:T(8,128)(2,1)}) %all-gather.12.cloned.1.call-update) | async-done | bytes 4194320 | tf_op jit(solution)/shard_map/all_gather | solution.py:23
  68.7 3.1 fusion.1
  71.8 77.9 %all-gather.14.cloned.1.call-done = bf16[4096,1024]{1,0:T(8,128)(2,1)} async-done(((bf16[512,1024]{1,0:T(8,128)(2,1)}), bf16[4096,1024]{1,0:T(8,128)(2,1)}) %all-gather.14.cloned.1.call-update) | async-done | bytes 8388624 | tf_op jit(solution)/shard_map/all_gather | solution.py:86
  149.7 9.2 %convolution_convert_fusion.4 = bf16[512,1024]{1,0:T(8,128)(2,1)S(1)} fusion(bf16[4096,1024]{1,0:T(8,128)(2,1)} %all-gather.14.cloned.1.call-done, bf16[512,4096]{1,0:T(8,128)(2,1)} %all-gather.12.cloned.1.call-done, f32[4096]{0:T(1024)S(1)} %mul.72, f32[512]{0:T(512)S(1)} %add_rsqrt_fusion.1), kind=kOutput, calls=%fused_computation.21 | convolution fusion | flops 4303880192 | bytes 13649920 | tf_op jit(solution)/shard_map/dot_general | solution.py:39
  158.9 1.0 reshape.107
  159.9 72.0 %all-gather.18.cloned.1.call-done = bf16[4096,1024]{1,0:T(8,128)(2,1)} async-done(((bf16[512,1024]{1,0:T(8,128)(2,1)}), bf16[4096,1024]{1,0:T(8,128)(2,1)}) %all-gather.18.cloned.1.call-update) | async-done | bytes 8388624 | tf_op jit(solution)/shard_map/all_gather | solution.py:85
  231.9 9.2 %convolution_convert_fusion.2 = bf16[512,1024]{1,0:T(8,128)(2,1)S(1)} fusion(bf16[4096,1024]{1,0:T(8,128)(2,1)} %all-gather.18.cloned.1.call-done, bf16[512,4096]{1,0:T(8,128)(2,1)} %all-gather.12.cloned.1.call-done, f32[4096]{0:T(1024)S(1)} %mul.72, f32[512]{0:T(512)S(1)} %add_rsqrt_fusion.1), kind=kOutput, calls=%fused_computation.19 | convolution fusion | flops 4303880192 | bytes 13649920 | tf_op jit(solution)/shard_map/dot_general | solution.py:39
  241.1 0.8 reshape.109
  241.9 72.1 %all-gather.16.cloned.1.call-done = bf16[4096,1024]{1,0:T(8,128)(2,1)} async-done(((bf16[512,1024]{1,0:T(8,128)(2,1)}), bf16[4096,1024]{1,0:T(8,128)(2,1)}) %all-gather.16.cloned.1.call-update) | async-done | bytes 8388624 | tf_op jit(solution)/shard_map/all_gather | solution.py:84
  314.0 10.2 %convolution_convert_fusion.3 = bf16[512,1024]{1,0:T(8,128)(2,1)} fusion(bf16[4096,1024]{1,0:T(8,128)(2,1)} %all-gather.16.cloned.1.call-done, bf16[512,4096]{1,0:T(8,128)(2,1)} %all-gather.12.cloned.1.call-done, f32[4096]{0:T(1024)S(1)} %mul.72, f32[512]{0:T(512)S(1)} %add_rsqrt_fusion.1), kind=kOutput, calls=%fused_computation.20 | convolution fusion | flops 4303880192 | bytes 13649920 | tf_op jit(solution)/shard_map/dot_general | solution.py:39
  324.2 1.9 reshape.108
  326.1 0.9 fusion.37
  326.9 1.9 fusion.12
  328.8 3.6 fusion.8
  332.4 1.7 copy.27
  334.2 1.2 copy.31
  335.4 0.3 all-gather.24.cloned.1.call-start
  335.7 60.4 %all-gather.22.cloned.1.call-done = bf16[4096,1024]{1,0:T(8,128)(2,1)} async-done(((bf16[512,1024]{1,0:T(8,128)(2,1)}), bf16[4096,1024]{1,0:T(8,128)(2,1)}) %all-gather.22.cloned.1.call-update) | async-done | bytes 8388624 | tf_op jit(solution)/shard_map/all_gather | solution.py:96
  396.1 56.3 %all-gather.20.cloned.1.call-done = bf16[512,4096]{1,0:T(8,128)(2,1)} async-done(((bf16[512,1024]{1,0:T(8,128)(2,1)}), bf16[512,4096]{1,0:T(8,128)(2,1)}) %all-gather.20.cloned.1.call-update) | async-done | bytes 4194320 | tf_op jit(solution)/shard_map/all_gather | solution.py:95
  452.4 10.1 %add_convert_fusion = bf16[512,1024]{1,0:T(8,128)(2,1)} fusion(bf16[512,1024]{1,0:T(8,128)(2,1)S(1)} %copy-done, bf16[512,4096]{1,0:T(8,128)(2,1)} %all-gather.20.cloned.1.call-done, bf16[4096,1024]{1,0:T(8,128)(2,1)} %all-gather.22.cloned.1.call-done), kind=kOutput, calls=%fused_computation.12 | convolution fusion | flops 4296540160 | bytes 14680064 | tf_op jit(solution)/shard_map/dot_general | solution.py:39
  462.5 0.0 all-gather.26.cloned.1.call-start
  462.5 0.7 all-gather.26.cloned.1.call-update
  463.2 0.0 all-gather.28.cloned.1.call-start
  463.3 0.7 all-gather.28.cloned.1.call-update
  464.0 8.0 %all-gather.1 = bf16[4096]{0:T(1024)(128)(2,1)S(1)} all-gather(bf16[1024]{0:T(1024)(128)(2,1)S(1)} %copy-done.2), channel_id=3, replica_groups=mesh['row'=8,'col'=4] {'col'}, dimensions={0}, use_global_device_ids=true | all-gather | bytes 10240 | tf_op jit(solution)/shard_map/all_gather | solution.py:29
  472.0 43.3 %all-gather.24.cloned.1.call-done = bf16[512,4096]{1,0:T(8,128)(2,1)} async-done(((bf16[512,1024]{1,0:T(8,128)(2,1)}), bf16[512,4096]{1,0:T(8,128)(2,1)}) %all-gather.24.cloned.1.call-update) | async-done | bytes 4194320 | tf_op jit(solution)/shard_map/all_gather | solution.py:28
  515.4 3.1 fusion.4
  518.4 77.9 %all-gather.26.cloned.1.call-done = bf16[4096,1024]{1,0:T(8,128)(2,1)} async-done(((bf16[512,1024]{1,0:T(8,128)(2,1)}), bf16[4096,1024]{1,0:T(8,128)(2,1)}) %all-gather.26.cloned.1.call-update) | async-done | bytes 8388624 | tf_op jit(solution)/shard_map/all_gather | solution.py:102
  596.3 9.2 %convolution_convert_fusion.1 = bf16[512,1024]{1,0:T(8,128)(2,1)S(1)} fusion(bf16[4096,1024]{1,0:T(8,128)(2,1)} %all-gather.26.cloned.1.call-done, bf16[512,4096]{1,0:T(8,128)(2,1)} %all-gather.24.cloned.1.call-done, f32[4096]{0:T(1024)S(1)} %mul.73, f32[512]{0:T(512)S(1)} %add_rsqrt_fusion), kind=kOutput, calls=%fused_computation.18 | convolution fusion | flops 4303880192 | bytes 13649920 | tf_op jit(solution)/shard_map/dot_general | solution.py:39
  605.5 1.6 reshape.112
  607.1 71.5 %all-gather.28.cloned.1.call-done = bf16[4096,1024]{1,0:T(8,128)(2,1)} async-done(((bf16[512,1024]{1,0:T(8,128)(2,1)}), bf16[4096,1024]{1,0:T(8,128)(2,1)}) %all-gather.28.cloned.1.call-update) | async-done | bytes 8388624 | tf_op jit(solution)/shard_map/all_gather | solution.py:103
  678.5 9.2 %convolution_convert_fusion = bf16[512,1024]{1,0:T(8,128)(2,1)S(1)} fusion(bf16[4096,1024]{1,0:T(8,128)(2,1)} %all-gather.28.cloned.1.call-done, bf16[512,4096]{1,0:T(8,128)(2,1)} %all-gather.24.cloned.1.call-done, f32[4096]{0:T(1024)S(1)} %mul.73, f32[512]{0:T(512)S(1)} %add_rsqrt_fusion), kind=kOutput, calls=%fused_computation.17 | convolution fusion | flops 4303880192 | bytes 13649920 | tf_op jit(solution)/shard_map/dot_general | solution.py:39
  687.7 1.6 reshape.113
  (19 shorter events, 0.2 us)
Async XLA Ops:
  7.2 61.6 %all-gather.12.cloned.1.call-start = ((), (), s32[]{:S(2)}) async-start(), calls=%async_computation | async-start | bytes 5242880 | tf_op jit(solution)/shard_map/all_gather | solution.py:23
  13.7 3.9 copy-start.1
  13.7 12.0 %copy-start.3 = (s32[2]{0:T(128)S(1)}, s32[2]{0:T(128)}, u32[]{:S(2)}) copy-start(s32[2]{0:T(128)} %param.12) | copy-start | bytes 28
  14.9 134.8 %all-gather.14.cloned.1.call-start = ((), (), s32[]{:S(2)}) async-start(), calls=%async_computation.1 | async-start | bytes 9437184 | tf_op jit(solution)/shard_map/all_gather | solution.py:86
  15.7 216.3 %all-gather.18.cloned.1.call-start = ((), (), s32[]{:S(2)}) async-start(), calls=%async_computation.3 | async-start | bytes 9437184 | tf_op jit(solution)/shard_map/all_gather | solution.py:85
  16.4 297.6 %all-gather.16.cloned.1.call-start = ((), (), s32[]{:S(2)}) async-start(), calls=%async_computation.2 | async-start | bytes 9437184 | tf_op jit(solution)/shard_map/all_gather | solution.py:84
  17.0 379.1 %all-gather.22.cloned.1.call-start = ((), (), s32[]{:S(2)}) async-start(), calls=%async_computation.5 | async-start | bytes 9437184 | tf_op jit(solution)/shard_map/all_gather | solution.py:96
  17.6 434.8 %all-gather.20.cloned.1.call-start = ((), (), s32[]{:S(2)}) async-start(), calls=%async_computation.4 | async-start | bytes 5242880 | tf_op jit(solution)/shard_map/all_gather | solution.py:95
  332.4 119.9 %copy-start = (bf16[512,1024]{1,0:T(8,128)(2,1)S(1)}, bf16[512,1024]{1,0:T(8,128)(2,1)}, u32[]{:S(2)}) copy-start(bf16[512,1024]{1,0:T(8,128)(2,1)} %broadcast_select_fusion) | copy-start | bytes 3145732
  335.4 128.6 %copy-start.2 = (bf16[1024]{0:T(1024)(128)(2,1)S(1)}, bf16[1024]{0:T(1024)(128)(2,1)}, u32[]{:S(2)}) copy-start(bf16[1024]{0:T(1024)(128)(2,1)} %param.15) | copy-start | bytes 6148
  335.4 179.9 %all-gather.24.cloned.1.call-start = ((), (), s32[]{:S(2)}) async-start(), calls=%async_computation.6 | async-start | bytes 5242880 | tf_op jit(solution)/shard_map/all_gather | solution.py:28
  462.5 133.8 %all-gather.26.cloned.1.call-start = ((), (), s32[]{:S(2)}) async-start(), calls=%async_computation.7 | async-start | bytes 9437184 | tf_op jit(solution)/shard_map/all_gather | solution.py:102
  463.2 215.3 %all-gather.28.cloned.1.call-start = ((), (), s32[]{:S(2)}) async-start(), calls=%async_computation.8 | async-start | bytes 9437184 | tf_op jit(solution)/shard_map/all_gather | solution.py:103
Sparse Core Ops, SparseCore 0:
  15.0 53.6 all-gather.11
  70.3 79.3 all-gather.13
  151.3 80.5 all-gather.17
  233.4 80.5 all-gather.15
  315.5 80.5 all-gather.21
  398.4 53.9 all-gather.19
  462.6 52.6 all-gather.23
  517.0 79.3 all-gather.25
  597.9 80.5 all-gather.27
where the time goes:
time: 701 us; the launch traced here: 696 us
  waiting for transfers between devices  578 us (82%)
  matrix products  63.4 us (9%)
  local copies, waits for them, and re-layouts  16.3 us (2%)
  blocking collectives  16.1 us (2%)
  between operations  14 us (2%)
  other arithmetic  7.42 us (1%)
    all_gather x2, waiting for transfers between devices, spread_norm(): lax.all_gather(row_block, 'col', axis=1, tiled=True)  86.3 us
    all_gather x1, waiting for transfers between devices, shards(): lax.all_gather(value_weight, 'row', axis=0, tiled=True)  77.9 us
    all_gather x1, waiting for transfers between devices, shards(): lax.all_gather(crosskey_weight, 'row', axis=0, tiled=True)  77.9 us
    all_gather x1, waiting for transfers between devices, shards(): lax.all_gather(query_weight, 'row', axis=0, tiled=True)  72.1 us
    all_gather x1, waiting for transfers between devices, shards(): lax.all_gather(key_weight, 'row', axis=0, tiled=True)  72 us
    all_gather x1, waiting for transfers between devices, shards(): lax.all_gather(crossvalue_weight, 'row', axis=0, tiled=True)  71.5 us
    all_gather x1, waiting for transfers between devices, shards(): lax.all_gather(out_weight, 'row', axis=0, tiled=True)  60.4 us
    dot_general x6, matrix products, add_terms(): jnp.dot(source, weight_piece, preferred_element_type=jnp.float32)  57 us
  transfers between devices with their start and end apart: 9, of which 9 were waited for; matrix products, arithmetic and copies ran while one was open for 8% of the time, Pallas kernels for 0%

commit v1 on v0

--- a/solution.py
+++ b/solution.py
@@ -1,6 +1,10 @@
 import jax
 import jax.numpy as jnp
+import functools
+
 from jax import lax
+from jax.experimental import pallas as pl
+from jax.experimental.pallas import tpu as pltpu
 from jax.sharding import PartitionSpec as P
 
 D = 4096
@@ -109,9 +113,406 @@
     return (hidden_out, cross_keys, cross_values)
 
 
+def remote(source, target, send_sem, recv_sem, device):
+    return pltpu.make_async_remote_copy(
+        src_ref=source,
+        dst_ref=target,
+        send_sem=send_sem,
+        recv_sem=recv_sem,
+        device_id=device,
+        device_id_type=pl.DeviceIdType.MESH,
+    )
+
+
+def place_here():
+    row, col = lax.axis_index("row"), lax.axis_index("col")
+    near = col + 1 - 2 * lax.rem(col, 2)
+    far = lax.rem(col + 2, 4)
+    return row, col, near, far
+
+
+def greet(devices):
+    barrier = pltpu.get_barrier_semaphore()
+    for device in devices:
+        pl.semaphore_signal(
+            barrier, inc=1, device_id=device, device_id_type=pl.DeviceIdType.MESH
+        )
+    pl.semaphore_wait(barrier, len(devices))
+
+
+def first_hop(item, block, place, sends, recvs):
+    row, col, near, far = place_here()
+    copies = [
+        remote(block, place(col), sends.at[item, 0], recvs.at[item, 0], (row, near)),
+        remote(block, place(col), sends.at[item, 1], recvs.at[item, 1], (row, far)),
+    ]
+    for copy in copies:
+        copy.start()
+    return copies
+
+
+def second_hop(item, first, half, sends, recvs):
+    row, col, near, far = place_here()
+    first[0].wait_recv()
+    upper = remote(
+        half(near, 0), half(near, 0), sends.at[item, 2], recvs.at[item, 2], (row, far)
+    )
+    upper.start()
+    first[1].wait_recv()
+    lower = remote(
+        half(far, 1), half(far, 1), sends.at[item, 3], recvs.at[item, 3], (row, near)
+    )
+    lower.start()
+    return [upper, lower]
+
+
+def settle(first, second):
+    for copy in second:
+        copy.wait()
+    for copy in first:
+        copy.wait_send()
+
+
+def row_places(full_ref, start, rows, width):
+    def place(col):
+        return full_ref.at[pl.ds(start, rows), pl.ds(pl.multiple_of(col * width, width), width)]
+
+    def half(col, which):
+        return full_ref.at[
+            pl.ds(start + which * (rows // 2), rows // 2),
+            pl.ds(pl.multiple_of(col * width, width), width),
+        ]
+
+    return place, half
+
+
+def spread_kernel(
+    planes,
+    parts,
+    x_ref,
+    q_ref,
+    k_ref,
+    v_ref,
+    full_ref,
+    weight_ref,
+    local_sem,
+    sends,
+    recvs,
+    plane_send,
+    plane_recv,
+    core_send,
+    core_recv,
+):
+    row, col, near, far = place_here()
+    plane, core = row // 2, lax.rem(row, 2)
+    other = row + 1 - 2 * core
+    others = [2 * lax.rem(plane + step, planes) + core for step in range(1, planes)]
+    greet([(row, near), (row, far), (other, col)] + [(there, col) for there in others])
+
+    rows, width = x_ref.shape
+    depth = q_ref.shape[0]
+    head_width = q_ref.shape[1] // planes
+    chunk = rows // parts
+    sources = (q_ref, k_ref, v_ref)
+
+    def weight_rows(owner):
+        return pl.ds(pl.multiple_of(owner * depth, depth), depth)
+
+    def piece(which, target):
+        return sources[which].at[
+            :, pl.ds(pl.multiple_of(target * head_width, head_width), head_width)
+        ]
+
+    def slot(which, owner):
+        return weight_ref.at[weight_rows(owner), pl.ds(which * head_width, head_width)]
+
+    firsts, halves = [], []
+    for part in range(parts):
+        place, half = row_places(full_ref, part * chunk, chunk, width)
+        firsts.append(
+            first_hop(part, x_ref.at[pl.ds(part * chunk, chunk), :], place, sends, recvs)
+        )
+        halves.append(half)
+    own = [
+        pltpu.make_async_copy(piece(which, plane), slot(which, row), local_sem.at[which])
+        for which in range(3)
+    ]
+    own.append(
+        pltpu.make_async_copy(
+            x_ref, full_ref.at[:, pl.ds(pl.multiple_of(col * width, width), width)], local_sem.at[3]
+        )
+    )
+    for copy in own:
+        copy.start()
+    crossing = []
+    for step in range(1, planes):
+        target = lax.rem(plane + step, planes)
+        crossing.append(
+            [
+                remote(
+                    piece(which, target),
+                    slot(which, row),
+                    plane_send.at[step - 1, which],
+                    plane_recv.at[step - 1, which],
+                    (2 * target + core, col),
+                )
+                for which in range(3)
+            ]
+        )
+        for copy in crossing[-1]:
+            copy.start()
+    seconds = []
+    for part in range(parts):
+        seconds.append(second_hop(part, firsts[part], halves[part], sends, recvs))
+    shared = []
+    for step in range(planes):
+        if step == 0:
+            for copy in own[:3]:
+                copy.wait()
+        else:
+            for copy in crossing[step - 1]:
+                copy.wait_recv()
+        owner = 2 * lax.rem(plane + planes - step, planes) + core
+        block = weight_ref.at[weight_rows(owner), :]
+        shared.append(remote(block, block, core_send.at[step], core_recv.at[step], (other, col)))
+        shared[-1].start()
+    own[3].wait()
+    for part in range(parts):
+        settle(firsts[part], seconds[part])
+    for group in crossing:
+        for copy in group:
+            copy.wait_send()
+    for copy in shared:
+        copy.wait()
+
+
+def spread(x, weights, planes):
+    rows, width = x.shape
+    depth, columns = weights[0].shape
+    parts = planes
+    head_width = columns // planes
+    return pl.pallas_call(
+        functools.partial(spread_kernel, planes, parts),
+        out_shape=(
+            jax.ShapeDtypeStruct((rows, 4 * width), x.dtype),
+            jax.ShapeDtypeStruct((2 * planes * depth, 3 * head_width), x.dtype),
+        ),
+        in_specs=[pl.BlockSpec(memory_space=pl.ANY)] * 4,
+        out_specs=[pl.BlockSpec(memory_space=pl.ANY)] * 2,
+        scratch_shapes=[
+            pltpu.SemaphoreType.DMA((4,)),
+            pltpu.SemaphoreType.DMA((parts, 4)),
+            pltpu.SemaphoreType.DMA((parts, 4)),
+            pltpu.SemaphoreType.DMA((planes - 1, 3)),
+            pltpu.SemaphoreType.DMA((planes - 1, 3)),
+            pltpu.SemaphoreType.DMA((planes,)),
+            pltpu.SemaphoreType.DMA((planes,)),
+        ],
+        compiler_params=pltpu.CompilerParams(collective_id=0, has_side_effects=True),
+        cost_estimate=pl.CostEstimate(
+            flops=0, bytes_accessed=20 * rows * width * 2, transcendentals=0
+        ),
+    )(x, *weights)
+
+
+def regroup_kernel(
+    planes, att_ref, full_ref, local_sem, sends, recvs, plane_send, plane_recv
+):
+    row, col, near, far = place_here()
+    plane, core = row // 2, lax.rem(row, 2)
+    others = [2 * lax.rem(plane + step, planes) + core for step in range(1, planes)]
+    greet([(row, near), (row, far)] + [(there, col) for there in others])
+
+    rows, head_width = att_ref.shape
+    rows = rows // planes
+    width = head_width * planes
+
+    def block(target):
+        return att_ref.at[pl.ds(pl.multiple_of(target * rows, rows), rows), :]
+
+    def places(source):
+        def columns(where):
+            return pl.ds(
+                pl.multiple_of(where * width + source * head_width, head_width), head_width
+            )
+
+        def place(where):
+            return full_ref.at[:, columns(where)]
+
+        def half(where, which):
+            return full_ref.at[pl.ds(which * (rows // 2), rows // 2), columns(where)]
+
+        return place, half
+
+    crossing = []
+    for step in range(1, planes):
+        target = lax.rem(plane + step, planes)
+        crossing.append(
+            remote(
+                block(target),
+                places(plane)[0](col),
+                plane_send.at[step - 1],
+                plane_recv.at[step - 1],
+                (2 * target + core, col),
+            )
+        )
+        crossing[-1].start()
+    own = pltpu.make_async_copy(block(plane), places(plane)[0](col), local_sem.at[0])
+    own.start()
+    firsts, halves = [], []
+    for step in range(planes):
+        place, half = places(lax.rem(plane + planes - step, planes))
+        if step > 0:
+            crossing[step - 1].wait_recv()
+            start = place(col)
+        else:
+            start = block(plane)
+        firsts.append(first_hop(step, start, place, sends, recvs))
+        halves.append(half)
+    seconds = []
+    for step in range(planes):
+        seconds.append(second_hop(step, firsts[step], halves[step], sends, recvs))
+    own.wait()
+    for step in range(planes):
+        settle(firsts[step], seconds[step])
+    for copy in crossing:
+        copy.wait_send()
+
+
+def regroup(attended, planes):
+    rows, head_width = attended.shape
+    return pl.pallas_call(
+        functools.partial(regroup_kernel, planes),
+        out_shape=jax.ShapeDtypeStruct(
+            (rows // planes, 4 * planes * head_width), attended.dtype
+        ),
+        in_specs=[pl.BlockSpec(memory_space=pl.ANY)],
+        out_specs=pl.BlockSpec(memory_space=pl.ANY),
+        scratch_shapes=[
+            pltpu.SemaphoreType.DMA((1,)),
+            pltpu.SemaphoreType.DMA((planes, 4)),
+            pltpu.SemaphoreType.DMA((planes, 4)),
+            pltpu.SemaphoreType.DMA((planes - 1,)),
+            pltpu.SemaphoreType.DMA((planes - 1,)),
+        ],
+        compiler_params=pltpu.CompilerParams(collective_id=1, has_side_effects=True),
+        cost_estimate=pl.CostEstimate(
+            flops=0, bytes_accessed=40 * rows * head_width * 2, transcendentals=0
+        ),
+    )(attended)
+
+
+def widen_kernel(parts, x_ref, full_ref, local_sem, sends, recvs):
+    row, col, near, far = place_here()
+    greet([(row, near), (row, far)])
+    rows, width = x_ref.shape
+    chunk = rows // parts
+    firsts, halves = [], []
+    for part in range(parts):
+        place, half = row_places(full_ref, part * chunk, chunk, width)
+        firsts.append(
+            first_hop(part, x_ref.at[pl.ds(part * chunk, chunk), :], place, sends, recvs)
+        )
+        halves.append(half)
+    own = pltpu.make_async_copy(
+        x_ref, full_ref.at[:, pl.ds(pl.multiple_of(col * width, width), width)], local_sem.at[0]
+    )
+    own.start()
+    seconds = []
+    for part in range(parts):
+        seconds.append(second_hop(part, firsts[part], halves[part], sends, recvs))
+    own.wait()
+    for part in range(parts):
+        settle(firsts[part], seconds[part])
+
+
+def widen(x, parts=4):
+    rows, width = x.shape
+    return pl.pallas_call(
+        functools.partial(widen_kernel, parts),
+        out_shape=jax.ShapeDtypeStruct((rows, 4 * width), x.dtype),
+        in_specs=[pl.BlockSpec(memory_space=pl.ANY)],
+        out_specs=pl.BlockSpec(memory_space=pl.ANY),
+        scratch_shapes=[
+            pltpu.SemaphoreType.DMA((1,)),
+            pltpu.SemaphoreType.DMA((parts, 4)),
+            pltpu.SemaphoreType.DMA((parts, 4)),
+        ],
+        compiler_params=pltpu.CompilerParams(collective_id=2, has_side_effects=True),
+        cost_estimate=pl.CostEstimate(
+            flops=0, bytes_accessed=20 * rows * width * 2, transcendentals=0
+        ),
+    )(x)
+
+
+def norm_rows(gathered, gains):
+    widened = gathered.astype(jnp.float32)
+    summed = jnp.sum(widened * widened, axis=1, keepdims=True)
+    return scaled_rows(widened, summed, gains)
+
+
+def plane_shards(
+    planes,
+    token_ids,
+    passage_lengths,
+    embedding,
+    attn_gain,
+    final_gain,
+    query_weight,
+    key_weight,
+    value_weight,
+    out_weight,
+    crosskey_weight,
+    crossvalue_weight,
+):
+    row = lax.axis_index("row")
+    plane, core = row // 2, row % 2
+    tok_rows = token_ids.size
+    local_width = query_weight.shape[1]
+    facts = jnp.concatenate([token_ids.reshape(-1), passage_lengths])
+    facts = lax.all_gather(facts, "row", axis=0).reshape(planes, 2, -1)
+    facts = lax.dynamic_index_in_dim(facts, core, axis=1, keepdims=False)
+    ids, lengths = facts[:, :tok_rows].reshape(-1), facts[:, tok_rows:].reshape(-1)
+    gains = lax.all_gather(jnp.concatenate([attn_gain, final_gain]), "col", axis=0)
+    gains = gains.reshape(4, 2, -1).transpose(1, 0, 2).reshape(2, 1, -1)
+
+    embedded_all = jnp.take(embedding, ids, axis=0)
+    embedded = lax.dynamic_slice_in_dim(embedded_all, plane * tok_rows, tok_rows, axis=0)
+    gathered, weight = spread(embedded_all, (query_weight, key_weight, value_weight), planes)
+    normed = norm_rows(gathered, gains[0])
+    (sums,) = add_terms(normed, (weight,))
+    sums = sums.astype(jnp.bfloat16)
+    part = local_width // planes
+    attended = attend(sums[:, :part], sums[:, part : 2 * part], sums[:, 2 * part :], lengths)
+    heads_full = regroup(attended, planes)
+    (projected,) = add_terms(heads_full, (lax.all_gather(out_weight, "row", axis=0, tiled=True),))
+    hidden_out = (embedded.astype(jnp.float32) + projected).astype(jnp.bfloat16)
+    final_normed = norm_rows(widen(hidden_out), gains[1])
+    crosskey_sum, crossvalue_sum = add_terms(
+        final_normed,
+        (
+            lax.all_gather(crosskey_weight, "row", axis=0, tiled=True),
+            lax.all_gather(crossvalue_weight, "row", axis=0, tiled=True),
+        ),
+    )
+    heads_here = local_width // HD
+    cross_keys = crosskey_sum.astype(jnp.bfloat16).reshape(tok_rows, heads_here, HD)
+    cross_values = crossvalue_sum.astype(jnp.bfloat16).reshape(tok_rows, heads_here, HD)
+    return (hidden_out, cross_keys, cross_values)
+
+
+def any_shards(mesh):
+    rows, cols = mesh.shape["row"], mesh.shape["col"]
+    planes = rows // 2
+    heads_here = D // HD // cols
+    if cols == 4 and rows % 2 == 0 and planes > 1 and heads_here % planes == 0:
+        return functools.partial(plane_shards, planes)
+    return shards
+
+
 def solution(mesh):
     return jax.shard_map(
-        shards,
+        any_shards(mesh),
         mesh=mesh,
         in_specs=(
             P("row", None),

time: 701 us -> 433 us (0.62)
  waiting for transfers between devices: 578 us -> 2.1 us
  Pallas kernels: 0 us -> 263 us
  local copies, waits for them, and re-layouts: 16.3 us -> 49.7 us
  blocking collectives: 16.1 us -> 33.3 us
  matrix products: 63.4 us -> 53 us
  other arithmetic: 7.42 us -> 16.1 us
    all_gather x9 -> x3, waiting for transfers between devices: 574 us -> 0.04 us  [the longest x1 0.02 us: plane_shards(): lax.all_gather(out_weight, 'row', axis=0, tiled=True)]
    pallas_call x0 -> x3, Pallas kernels: none -> 263 us  [the longest x1 158 us: spread(): pl.pallas_call(functools.partial(spread_kernel, planes, parts), out_shape...]
    gather x1, local copies, waits for them, and re-layouts: 5.11 us -> 40.8 us  [plane_shards(): embedded_all = jnp.take(embedding, ids, axis=0)]
    unnamed x0 -> x1, blocking collectives: none -> 25 us
    dot_general x6 -> x4, matrix products: 57 us -> 46.4 us  [add_terms(): jnp.dot(source, weight_piece, preferred_element_type=jnp.float32)]
    all_gather x2 -> x1, blocking collectives: 16.1 us -> 8.21 us  [plane_shards(): lax.all_gather(jnp.concatenate([attn_gain, final_gain]), 'col', axis=0)]
  transfers between devices with their start and end apart: 9 -> 3, of which waited for: 9 -> 0; matrix products, arithmetic and copies ran while one was open for 8% -> 24% of each run, Pallas kernels for 0% -> 61%
where the time goes in v1:
time: 433 us; the launch traced here: 432 us
  Pallas kernels  263 us (61%)
  matrix products  53 us (12%)
  local copies, waits for them, and re-layouts  49.7 us (11%)
  blocking collectives  33.3 us (8%)
  other arithmetic  16.1 us (4%)
  between operations  14.6 us (3%)
    pallas_call x1, Pallas kernels, spread(): pl.pallas_call(functools.partial(spread_kernel, planes, parts), out_shape...  158 us
    pallas_call x1, Pallas kernels, regroup(): pl.pallas_call(functools.partial(regroup_kernel, planes), out_shape=jax.S...  71.6 us
    dot_general x4, matrix products, add_terms(): jnp.dot(source, weight_piece, preferred_element_type=jnp.float32)  46.4 us
    gather x1, local copies, waits for them, and re-layouts, plane_shards(): embedded_all = jnp.take(embedding, ids, axis=0)  40.8 us
    pallas_call x1, Pallas kernels, widen(): pl.pallas_call(functools.partial(widen_kernel, parts), out_shape=jax.Shap...  33.9 us
    unnamed x1, blocking collectives  25 us
    reduce_sum x2, other arithmetic, norm_rows(): summed = jnp.sum(widened * widened, axis=1, keepdims=True)  10.6 us
  transfers between devices with their start and end apart: 3, of which 0 were waited for; matrix products, arithmetic and copies ran while one was open for 24% of the time, Pallas kernels for 61%

profile of v1, /device:TPU:24, one launch (start us, length us, event | category | flops | bytes accessed | tf_op | source)
XLA Modules:
  0.0 431.9 jit_solution(13291522158032773293)
XLA Ops:
  7.2 0.0 all-gather.6.cloned.1.call-start
  7.2 0.7 all-gather.6.cloned.1.call-update
  7.9 0.0 all-gather.10.cloned.1.call-start
  7.9 0.7 all-gather.10.cloned.1.call-update
  8.6 0.0 all-gather.8.cloned.1.call-start
  8.7 0.7 all-gather.8.cloned.1.call-update
  9.4 0.7 copy.19
  10.1 1.2 dynamic-slice
  12.0 0.8 add_dynamic-update-slice_fusion
  12.8 0.1 reshape.161
  12.9 25.0 %all-reduce.1 = s32[4,2,514]{2,1,0:T(2,128)S(1)} all-reduce(s32[4,2,514]{2,1,0:T(2,128)S(1)} %reshape.161), channel_id=2, replica_groups=mesh['row'=8,'col'=4] {'row'}, use_global_device_ids=true, to_apply=%add | all-reduce | flops 4112 | bytes 32896
  38.0 0.7 pad_maximum_fusion
  38.7 8.2 %all-gather.1 = bf16[8192]{0:T(1024)(128)(2,1)S(1)} all-gather(bf16[2048]{0:T(1024)(128)(2,1)S(1)} %pad_maximum_fusion), channel_id=3, replica_groups=mesh['row'=8,'col'=4] {'col'}, dimensions={0}, use_global_device_ids=true | all-gather | bytes 20480 | tf_op jit(solution)/shard_map/all_gather | solution.py:476
  46.9 0.1 lt.61
  47.0 40.8 %gather_fusion = bf16[2048,1024]{1,0:T(8,128)(2,1)} fusion(bf16[16384,1024]{1,0:T(8,128)(2,1)} %param.13, s32[2048]{0:T(1024)S(1)} %broadcast_clamp_fusion), kind=kCustom, calls=%fused_computation | custom fusion | bytes 8396800 | tf_op jit(solution)/shard_map/jit(_take)/gather | solution.py:479
  87.8 3.8 broadcast_select_fusion.x_ref
  91.6 157.5 %shard_map.130 = (bf16[2048,4096]{1,0:T(8,128)(2,1)}, bf16[4096,768]{1,0:T(8,128)(2,1)}) custom-call(bf16[2048,1024]{1,0:T(8,128)(2,1)} %broadcast_select_fusion.x_ref, bf16[512,1024]{1,0:T(8,128)(2,1)} %q_ref.1, bf16[512,1024]{1,0:T(8,128)(2,1)} %k_ref.1, bf16[512,1024]{1,0:T(8,128)(2,1)} %v_ref.1), custom_call_target="tpu_custom_call" | custom-call | bytes 83886080 | tf_op jit(solution)/shard_map/pallas_call | solution.py:294
  249.2 0.1 iota_compare_fusion
  249.2 0.0 copy-start
  249.2 7.6 %fusion.1 = f32[2048]{0:T(1024)S(1)} fusion(bf16[2048,4096]{1,0:T(8,128)(2,1)} %get-tuple-element.5), kind=kLoop, calls=%fused_computation.4 | loop fusion | flops 25163776 | bytes 16785408 | tf_op jit(solution)/shard_map/reduce_sum | solution.py:450
  256.8 3.4 copy-done
  260.2 17.7 %fusion.11 = bf16[2048,768]{1,0:T(8,128)(2,1)S(1)} fusion(bf16[4096,768]{1,0:T(8,128)(2,1)} %get-tuple-element.6, bf16[2048,4096]{1,0:T(8,128)(2,1)S(1)} %copy-done, f32[4096]{0:T(1024)S(1)} %bitcast.50, f32[2048]{0:T(1024)S(1)} %add_rsqrt_fusion), kind=kOutput, calls=%fused_computation.16 | convolution fusion | flops 12920029184 | bytes 26238976 | tf_op jit(solution)/shard_map/dot_general | solution.py:43
  278.0 0.2 fusion.30
  278.2 1.2 fusion.31
  279.4 1.8 fusion.32
  281.3 3.6 convolution_convert_fusion.2
  284.8 71.6 %shard_map.131 = bf16[512,4096]{1,0:T(8,128)(2,1)} custom-call(bf16[2048,256]{1,0:T(8,128)(2,1)} %bitcast.40), custom_call_target="tpu_custom_call" | custom-call | bytes 41943040 | tf_op jit(solution)/shard_map/pallas_call | solution.py:384
  356.5 0.0 all-gather.6.cloned.1.call-done
  356.5 10.3 %add_convert_fusion.x_ref = bf16[512,1024]{1,0:T(8,128)(2,1)} fusion(bf16[512,4096]{1,0:T(8,128)(2,1)} %shard_map.131, bf16[4096,1024]{1,0:T(8,128)(2,1)} %all-gather.6.cloned.1.call-done, bf16[2048,1024]{1,0:T(8,128)(2,1)} %broadcast_select_fusion.x_ref, s32[]{:T(128)S(6)} %select_n.49), kind=kOutput, calls=%fused_computation.17 | convolution fusion | flops 4296540160 | bytes 14680068 | tf_op jit(solution)/shard_map/dot_general | solution.py:43
  366.8 33.9 %shard_map.132 = bf16[512,4096]{1,0:T(8,128)(2,1)} custom-call(bf16[512,1024]{1,0:T(8,128)(2,1)} %add_convert_fusion.x_ref), custom_call_target="tpu_custom_call" | custom-call | bytes 20971520 | tf_op jit(solution)/shard_map/pallas_call | solution.py:431
  400.7 3.1 fusion.8
  403.8 0.0 all-gather.10.cloned.1.call-done
  403.8 9.2 %convolution_convert_fusion = bf16[512,1024]{1,0:T(8,128)(2,1)S(1)} fusion(bf16[4096,1024]{1,0:T(8,128)(2,1)} %all-gather.10.cloned.1.call-done, bf16[512,4096]{1,0:T(8,128)(2,1)} %shard_map.132, f32[4096]{0:T(1024)S(1)} %bitcast.48, f32[512]{0:T(512)S(1)} %add_rsqrt_fusion.1), kind=kOutput, calls=%fused_computation.22 | convolution fusion | flops 4303880192 | bytes 13649920 | tf_op jit(solution)/shard_map/dot_general | solution.py:43
  413.0 1.6 reshape.170
  414.6 0.0 all-gather.8.cloned.1.call-done
  414.6 9.2 %convolution_convert_fusion.1 = bf16[512,1024]{1,0:T(8,128)(2,1)S(1)} fusion(bf16[4096,1024]{1,0:T(8,128)(2,1)} %all-gather.8.cloned.1.call-done, bf16[512,4096]{1,0:T(8,128)(2,1)} %shard_map.132, f32[4096]{0:T(1024)S(1)} %bitcast.49, f32[512]{0:T(512)S(1)} %add_rsqrt_fusion.1), kind=kOutput, calls=%fused_computation.23 | convolution fusion | flops 4303880192 | bytes 13649920 | tf_op jit(solution)/shard_map/dot_general | solution.py:43
  423.8 1.6 reshape.169
  (14 shorter events, 0.1 us)
Async XLA Ops:
  7.2 349.3 %all-gather.6.cloned.1.call-start = ((), (), s32[]{:S(2)}) async-start(), calls=%async_computation | async-start | bytes 9437184 | tf_op jit(solution)/shard_map/all_gather | solution.py:488
  7.9 395.9 %all-gather.10.cloned.1.call-start = ((), (), s32[]{:S(2)}) async-start(), calls=%async_computation.2 | async-start | bytes 9437184 | tf_op jit(solution)/shard_map/all_gather | solution.py:495
  8.6 406.0 %all-gather.8.cloned.1.call-start = ((), (), s32[]{:S(2)}) async-start(), calls=%async_computation.1 | async-start | bytes 9437184 | tf_op jit(solution)/shard_map/all_gather | solution.py:494
  249.2 11.0 %copy-start = (bf16[2048,4096]{1,0:T(8,128)(2,1)S(1)}, bf16[2048,4096]{1,0:T(8,128)(2,1)}, u32[]{:S(2)}) copy-start(bf16[2048,4096]{1,0:T(8,128)(2,1)} %get-tuple-element.5) | copy-start | bytes 50331652
Sparse Core Ops, SparseCore 0:
  9.6 80.6 all-gather.5
  91.9 139.4 all-gather.9
  233.1 101.7 all-gather.7

commit v2 on v1

--- a/solution.py
+++ b/solution.py
@@ -445,6 +445,68 @@
     )(x)
 
 
+def announce_kernel(
+    planes, fact_ref, gain_ref, facts_ref, gains_ref, local_sem, sends, recvs, gain_send, gain_recv
+):
+    row, col, near, far = place_here()
+    plane, core = row // 2, lax.rem(row, 2)
+    rows = [(2 * lax.rem(plane + step, planes) + core, col) for step in range(1, planes)]
+    cols = [(row, near), (row, far), (row, 3 - col)]
+    greet(rows + cols)
+    tall, deep = fact_ref.shape[0], gain_ref.shape[0]
+    fact_slot = facts_ref.at[pl.ds(pl.multiple_of(plane * tall, tall), tall), :]
+    gain_slot = gains_ref.at[pl.ds(pl.multiple_of(col * deep, deep), deep), :]
+    copies = [
+        remote(fact_ref, fact_slot, sends.at[item], recvs.at[item], device)
+        for item, device in enumerate(rows)
+    ]
+    copies += [
+        remote(gain_ref, gain_slot, gain_send.at[item], gain_recv.at[item], device)
+        for item, device in enumerate(cols)
+    ]
+    copies += [
+        pltpu.make_async_copy(fact_ref, fact_slot, local_sem.at[0]),
+        pltpu.make_async_copy(gain_ref, gain_slot, local_sem.at[1]),
+    ]
+    for copy in copies:
+        copy.start()
+    for copy in copies:
+        copy.wait()
+
+
+def announce(token_ids, passage_lengths, attn_gain, final_gain, planes):
+    facts = jnp.concatenate([token_ids.reshape(-1), passage_lengths])
+    used = facts.shape[0]
+    facts = jnp.pad(facts, (0, -used % 1024)).reshape(-1, 128)
+    gains = jnp.concatenate([attn_gain, final_gain])
+    width = gains.shape[0]
+    gains = jnp.pad(gains, (0, -width % 2048)).reshape(-1, 128)
+    facts, gains = pl.pallas_call(
+        functools.partial(announce_kernel, planes),
+        out_shape=(
+            jax.ShapeDtypeStruct((planes * facts.shape[0], 128), facts.dtype),
+            jax.ShapeDtypeStruct((4 * gains.shape[0], 128), gains.dtype),
+        ),
+        in_specs=[pl.BlockSpec(memory_space=pl.ANY)] * 2,
+        out_specs=[pl.BlockSpec(memory_space=pl.ANY)] * 2,
+        scratch_shapes=[
+            pltpu.SemaphoreType.DMA((2,)),
+            pltpu.SemaphoreType.DMA((planes - 1,)),
+            pltpu.SemaphoreType.DMA((planes - 1,)),
+            pltpu.SemaphoreType.DMA((3,)),
+            pltpu.SemaphoreType.DMA((3,)),
+        ],
+        compiler_params=pltpu.CompilerParams(collective_id=3, has_side_effects=True),
+    )(facts, gains)
+    facts = facts.reshape(planes, -1)
+    gains = gains.reshape(4, -1)[:, :width].reshape(4, 2, -1)
+    return (
+        facts[:, : token_ids.size].reshape(-1),
+        facts[:, token_ids.size : used].reshape(-1),
+        gains.transpose(1, 0, 2).reshape(2, 1, -1),
+    )
+
+
 def norm_rows(gathered, gains):
     widened = gathered.astype(jnp.float32)
     summed = jnp.sum(widened * widened, axis=1, keepdims=True)
@@ -466,17 +528,11 @@
     crossvalue_weight,
 ):
     row = lax.axis_index("row")
-    plane, core = row // 2, row % 2
+    plane = row // 2
     tok_rows = token_ids.size
     local_width = query_weight.shape[1]
-    facts = jnp.concatenate([token_ids.reshape(-1), passage_lengths])
-    facts = lax.all_gather(facts, "row", axis=0).reshape(planes, 2, -1)
-    facts = lax.dynamic_index_in_dim(facts, core, axis=1, keepdims=False)
-    ids, lengths = facts[:, :tok_rows].reshape(-1), facts[:, tok_rows:].reshape(-1)
-    gains = lax.all_gather(jnp.concatenate([attn_gain, final_gain]), "col", axis=0)
-    gains = gains.reshape(4, 2, -1).transpose(1, 0, 2).reshape(2, 1, -1)
-
-    embedded_all = jnp.take(embedding, ids, axis=0)
+    ids, lengths, gains = announce(token_ids, passage_lengths, attn_gain, final_gain, planes)
+    embedded_all = jnp.take(embedding, ids, axis=0, mode="clip")
     embedded = lax.dynamic_slice_in_dim(embedded_all, plane * tok_rows, tok_rows, axis=0)
     gathered, weight = spread(embedded_all, (query_weight, key_weight, value_weight), planes)
     normed = norm_rows(gathered, gains[0])

time: 433 us -> 408 us (0.942)
  blocking collectives: 33.3 us -> 0 us
  Pallas kernels: 263 us -> 274 us
    unnamed x1 -> x0, blocking collectives: 25 us -> none
    all_gather x1 -> x0, blocking collectives: 8.21 us -> none  [plane_shards(): lax.all_gather(jnp.concatenate([attn_gain, final_gain]), 'col', axis=0)]
    pallas_call x1, Pallas kernels: 71.6 us -> 78 us  [regroup(): pl.pallas_call(functools.partial(regroup_kernel, planes), out_shape=jax.S...]
    pallas_call x0 -> x1, Pallas kernels: none -> 5.94 us  [announce(): pl.pallas_call(functools.partial(announce_kernel, planes), out_shape=(jax...]
  transfers between devices with their start and end apart: 3 -> 3, of which waited for: 0 -> 0; matrix products, arithmetic and copies ran while one was open for 24% -> 25% of each run, Pallas kernels for 61% -> 67%
where the time goes in v2:
time: 408 us; the launch traced here: 407 us
  Pallas kernels  274 us (67%)
  matrix products  53.1 us (13%)
  local copies, waits for them, and re-layouts  51.8 us (13%)
  between operations  13.9 us (3%)
  other arithmetic  12.7 us (3%)
    pallas_call x1, Pallas kernels, spread(): pl.pallas_call(functools.partial(spread_kernel, planes, parts), out_shape...  155 us
    pallas_call x1, Pallas kernels, regroup(): pl.pallas_call(functools.partial(regroup_kernel, planes), out_shape=jax.S...  78 us
    dot_general x4, matrix products, add_terms(): jnp.dot(source, weight_piece, preferred_element_type=jnp.float32)  46.4 us
    gather x1, local copies, waits for them, and re-layouts, plane_shards(): embedded_all = jnp.take(embedding, ids, axis=0, mode='clip')  42.3 us
    pallas_call x1, Pallas kernels, widen(): pl.pallas_call(functools.partial(widen_kernel, parts), out_shape=jax.Shap...  34.7 us
    reduce_sum x2, other arithmetic, norm_rows(): summed = jnp.sum(widened * widened, axis=1, keepdims=True)  10.6 us
  transfers between devices with their start and end apart: 3, of which 0 were waited for; matrix products, arithmetic and copies ran while one was open for 25% of the time, Pallas kernels for 67%

profile of v2, /device:TPU:24, one launch (start us, length us, event | category | flops | bytes accessed | tf_op | source)
XLA Modules:
  0.0 407.2 jit_solution(4004051616398388285)
XLA Ops:
  7.2 0.0 all-gather.4.cloned.1.call-start
  7.2 0.7 all-gather.4.cloned.1.call-update
  7.9 0.0 all-gather.6.cloned.1.call-start
  7.9 0.7 all-gather.6.cloned.1.call-update
  8.6 0.0 all-gather.8.cloned.1.call-start
  8.7 0.7 all-gather.8.cloned.1.call-update
  9.4 0.7 copy.17
  10.1 0.7 pad_add_fusion
  10.7 0.6 pad_bitcast_fusion.fact_ref
  11.3 1.3 pad_maximum_fusion.gain_ref
  12.6 5.9 %shard_map.130 = (s32[32,128]{1,0:T(8,128)}, bf16[64,128]{1,0:T(8,128)(2,1)}) custom-call(s32[8,128]{1,0:T(8,128)} %pad_bitcast_fusion.fact_ref, bf16[16,128]{1,0:T(8,128)(2,1)} %pad_maximum_fusion.gain_ref), custom_call_target="tpu_custom_call" | custom-call | tf_op jit(solution)/shard_map/pallas_call | solution.py:484
  18.6 0.7 reshape.128
  19.3 0.7 reshape_reshape.3
  20.1 0.1 lt.24
  20.2 42.3 %gather_fusion = bf16[2048,1024]{1,0:T(8,128)(2,1)} fusion(bf16[16384,1024]{1,0:T(8,128)(2,1)} %param.13, s32[2048]{0:T(1024)S(1)} %broadcast_clamp_fusion), kind=kCustom, calls=%fused_computation | custom fusion | bytes 8396800 | tf_op jit(solution)/shard_map/jit(_take)/gather | solution.py:535
  62.5 155.0 %shard_map.131 = (bf16[2048,4096]{1,0:T(8,128)(2,1)}, bf16[4096,768]{1,0:T(8,128)(2,1)}) custom-call(bf16[2048,1024]{1,0:T(8,128)(2,1)} %gather_fusion, bf16[512,1024]{1,0:T(8,128)(2,1)} %q_ref.1, bf16[512,1024]{1,0:T(8,128)(2,1)} %k_ref.1, bf16[512,1024]{1,0:T(8,128)(2,1)} %v_ref.1), custom_call_target="tpu_custom_call" | custom-call | bytes 83886080 | tf_op jit(solution)/shard_map/pallas_call | solution.py:294
  217.4 0.1 iota_compare_fusion
  217.5 0.0 copy-start
  217.5 7.5 %fusion.1 = f32[2048]{0:T(1024)S(1)} fusion(bf16[2048,4096]{1,0:T(8,128)(2,1)} %get-tuple-element.8), kind=kLoop, calls=%fused_computation.4 | loop fusion | flops 25163776 | bytes 16785408 | tf_op jit(solution)/shard_map/reduce_sum | solution.py:512
  225.1 3.3 copy-done
  228.4 17.7 %fusion.11 = bf16[2048,768]{1,0:T(8,128)(2,1)S(1)} fusion(bf16[4096,768]{1,0:T(8,128)(2,1)} %get-tuple-element.10, bf16[2048,4096]{1,0:T(8,128)(2,1)S(1)} %copy-done, f32[4096]{0:T(1024)S(1)} %bitcast.40, f32[2048]{0:T(1024)S(1)} %add_rsqrt_fusion), kind=kOutput, calls=%fused_computation.15 | convolution fusion | flops 12920029184 | bytes 26238976 | tf_op jit(solution)/shard_map/dot_general | solution.py:43
  246.1 0.2 fusion.30
  246.4 1.2 fusion.31
  247.6 1.8 fusion.32
  249.4 3.7 convolution_convert_fusion.2
  253.1 78.0 %shard_map.132 = bf16[512,4096]{1,0:T(8,128)(2,1)} custom-call(bf16[2048,256]{1,0:T(8,128)(2,1)} %bitcast.34), custom_call_target="tpu_custom_call" | custom-call | bytes 41943040 | tf_op jit(solution)/shard_map/pallas_call | solution.py:384
  331.0 0.0 all-gather.4.cloned.1.call-done
  331.1 10.3 %add_convert_fusion.x_ref = bf16[512,1024]{1,0:T(8,128)(2,1)} fusion(bf16[512,4096]{1,0:T(8,128)(2,1)} %shard_map.132, bf16[4096,1024]{1,0:T(8,128)(2,1)} %all-gather.4.cloned.1.call-done, bf16[2048,1024]{1,0:T(8,128)(2,1)} %gather_fusion, s32[]{:T(128)S(6)} %select_n.14), kind=kOutput, calls=%fused_computation.16 | convolution fusion | flops 4296540160 | bytes 14680068 | tf_op jit(solution)/shard_map/dot_general | solution.py:43
  341.3 34.7 %shard_map.133 = bf16[512,4096]{1,0:T(8,128)(2,1)} custom-call(bf16[512,1024]{1,0:T(8,128)(2,1)} %add_convert_fusion.x_ref), custom_call_target="tpu_custom_call" | custom-call | bytes 20971520 | tf_op jit(solution)/shard_map/pallas_call | solution.py:431
  376.0 3.1 fusion.8
  379.1 0.0 all-gather.6.cloned.1.call-done
  379.2 9.2 %convolution_convert_fusion.1 = bf16[512,1024]{1,0:T(8,128)(2,1)S(1)} fusion(bf16[4096,1024]{1,0:T(8,128)(2,1)} %all-gather.6.cloned.1.call-done, bf16[512,4096]{1,0:T(8,128)(2,1)} %shard_map.133, f32[4096]{0:T(1024)S(1)} %bitcast.38, f32[512]{0:T(512)S(1)} %add_rsqrt_fusion.1), kind=kOutput, calls=%fused_computation.22 | convolution fusion | flops 4303880192 | bytes 13649920 | tf_op jit(solution)/shard_map/dot_general | solution.py:43
  388.3 1.6 reshape.133
  389.9 0.0 all-gather.8.cloned.1.call-done
  389.9 9.2 %convolution_convert_fusion = bf16[512,1024]{1,0:T(8,128)(2,1)S(1)} fusion(bf16[4096,1024]{1,0:T(8,128)(2,1)} %all-gather.8.cloned.1.call-done, bf16[512,4096]{1,0:T(8,128)(2,1)} %shard_map.133, f32[4096]{0:T(1024)S(1)} %bitcast.39, f32[512]{0:T(512)S(1)} %add_rsqrt_fusion.1), kind=kOutput, calls=%fused_computation.21 | convolution fusion | flops 4303880192 | bytes 13649920 | tf_op jit(solution)/shard_map/dot_general | solution.py:43
  399.1 1.6 reshape.134
  (7 shorter events, 0.1 us)
Async XLA Ops:
  7.2 323.9 %all-gather.4.cloned.1.call-start = ((), (), s32[]{:S(2)}) async-start(), calls=%async_computation | async-start | bytes 9437184 | tf_op jit(solution)/shard_map/all_gather | solution.py:544
  7.9 371.2 %all-gather.6.cloned.1.call-start = ((), (), s32[]{:S(2)}) async-start(), calls=%async_computation.1 | async-start | bytes 9437184 | tf_op jit(solution)/shard_map/all_gather | solution.py:550
  8.6 381.3 %all-gather.8.cloned.1.call-start = ((), (), s32[]{:S(2)}) async-start(), calls=%async_computation.2 | async-start | bytes 9437184 | tf_op jit(solution)/shard_map/all_gather | solution.py:551
  217.5 10.9 %copy-start = (bf16[2048,4096]{1,0:T(8,128)(2,1)S(1)}, bf16[2048,4096]{1,0:T(8,128)(2,1)}, u32[]{:S(2)}) copy-start(bf16[2048,4096]{1,0:T(8,128)(2,1)} %get-tuple-element.8) | copy-start | bytes 50331652
Sparse Core Ops, SparseCore 0:
  9.6 101.0 all-gather.3
  112.3 112.7 all-gather.5
  226.7 102.6 all-gather.7
